TPU v7x, 512 devices: a whole 4x8x8 slice. The times are simulated.
512 devices in a mesh: dp: 64 (over y, z), tower: 8 (over x, core).
Axes of the slice: x: 4, y: 8, z: 8, core: 2. Of those that a mesh axis runs over, the one named last changes fastest.
Arguments:
- rep: bfloat16 [16384, 2048], P('dp', 'tower'), may hold values from -6 to 6
- arm_ids: int32 [16384], P('dp'), may hold values from 0 to 63, as said below
- outcome: bfloat16 [16384], P('dp'), may hold values from -6 to 6
- weight: bfloat16 [16384], P('dp'), may hold values from 0.5 to 4
- w_hidden: bfloat16 [64, 2048, 2048], P('dp', None, 'tower'), may hold values from -0.125 to 0.125
- b_hidden: float32 [64, 2048], P('dp', 'tower'), may hold values from -3 to 3
- w_head: float32 [64, 2048], P('dp', 'tower'), may hold values from -0.125 to 0.125
- b_head: float32 [64], P('dp'), may hold values from -4 to 4
Outputs:
- grad_hidden: float32 [64, 2048, 2048], P('dp', None, 'tower')
- grad_hidden_bias: float32 [64, 2048], P('dp', 'tower')
- grad_head: float32 [64, 2048], P('dp', 'tower')
- grad_head_bias: float32 [64], P('dp')
- grad_rep: bfloat16 [16384, 2048], P('dp', 'tower')
- predicted: bfloat16 [16384], P('dp')
Inputs may be any that keep to these rules, and one draw needn't show every extreme that they name: `arm_ids`: among the 256 rows of one index of dp at most 14 name one arm, and in every draw some index has an arm named exactly 14 times; over all 16384 rows at most 512 name one arm, and in every draw some arm is named exactly 512 times.
All inputs are finite; a program needn't handle non-finite values.
Results may differ from a plain program's by a relative error of at most 0.019.
Values may be sent and summed in bfloat16 or wider, within the bound.
No kernel may reach another device: no remote copies, remote signals or barrier semaphores. Data moves between devices by JAX's collectives and lax.ppermute only.
A program may use at most 64 MiB of HBM per device.

v0:
```python
import jax
import jax.numpy as jnp
from jax import lax
from jax.sharding import PartitionSpec as P


def arm_slots(arm_ids, arm_count, slot_depth):
    arm_labels = jnp.arange(arm_count, dtype=jnp.int32)
    one_hot = (arm_ids[:, None] == arm_labels[None, :]).astype(jnp.int32)
    arm_rank = jnp.sum(jnp.cumsum(one_hot, axis=0) * one_hot, axis=1) - 1
    return arm_ids * slot_depth + arm_rank


def fill_slots(values, slot_index, slot_total):
    row_count = values.shape[0]
    source_row = (
        jnp.full((slot_total,), row_count, jnp.int32)
        .at[slot_index]
        .set(jnp.arange(row_count, dtype=jnp.int32))
    )
    padded_rows = jnp.concatenate(
        [values, jnp.zeros((1,) + values.shape[1:], values.dtype)], axis=0
    )
    return padded_rows[source_row]


def tower_step(inputs, targets, weights, matrix, bias_cols, head_cols, head_bias):
    pre_act = jnp.dot(inputs, matrix, preferred_element_type=jnp.float32) + bias_cols
    sigmoid_pre = jax.nn.sigmoid(pre_act)
    activation = pre_act * sigmoid_pre
    pred_share = jnp.sum(activation * head_cols, axis=1)
    full_pred = lax.psum(pred_share, "tower") + head_bias
    resid_grad = weights * (full_pred - targets)
    pre_grad = resid_grad[:, None] * head_cols * sigmoid_pre * (1.0 + pre_act * (1.0 - sigmoid_pre))
    pre_grad_half = pre_grad.astype(jnp.bfloat16)
    grad_matrix = lax.dot_general(
        inputs, pre_grad_half, (((0,), (0,)), ((), ())), preferred_element_type=jnp.float32
    )
    grad_bias = jnp.sum(pre_grad, axis=0)
    grad_vector = jnp.sum(resid_grad[:, None] * activation, axis=0)
    grad_scalar = jnp.sum(resid_grad)
    return (full_pred, pre_grad_half, grad_matrix, grad_bias, grad_vector, grad_scalar)


def body(rep, arm_ids, outcome, weight, w_hidden, b_hidden, w_head, b_head):
    arm_count = lax.axis_size("dp")
    row_count = arm_ids.shape[0]
    slot_depth = 7 * (row_count // (2 * arm_count))
    slot_total = arm_count * slot_depth
    slot_index = arm_slots(arm_ids, arm_count, slot_depth)
    side_data = fill_slots(jnp.stack([outcome, weight], axis=1), slot_index, slot_total).reshape(
        arm_count, slot_depth, 2
    )
    matrix = w_hidden[0]
    bias_cols = b_hidden[0]
    head_cols = w_head[0]
    head_bias = b_head[0]
    wide_rep = lax.all_gather(rep, "tower", axis=1, tiled=True)
    wide_slots = fill_slots(wide_rep, slot_index, slot_total).reshape(
        arm_count, slot_depth, wide_rep.shape[1]
    )
    arrived, arrived_side = (
        lax.all_to_all(wide_slots, "dp", split_axis=0, concat_axis=0, tiled=True),
        lax.all_to_all(side_data, "dp", split_axis=0, concat_axis=0, tiled=True),
    )
    slot_rows = arrived.reshape(slot_total, arrived.shape[2])
    arrived_side = arrived_side.reshape(slot_total, 2).astype(jnp.float32)
    targets = arrived_side[:, 0]
    weights = arrived_side[:, 1]
    full_pred, pre_grad_half, grad_matrix, grad_bias, grad_vector, grad_scalar = tower_step(
        slot_rows, targets, weights, matrix, bias_cols, head_cols, head_bias
    )
    pred_half = full_pred.astype(jnp.bfloat16)
    partial_full = lax.dot_general(
        pre_grad_half, matrix, (((1,), (1,)), ((), ())), preferred_element_type=jnp.float32
    ).astype(jnp.bfloat16)
    full_width = partial_full.shape[1]
    returned, pred_back = (
        lax.all_to_all(
            partial_full.reshape(arm_count, slot_depth, full_width),
            "dp",
            split_axis=0,
            concat_axis=0,
            tiled=True,
        ),
        lax.all_to_all(
            pred_half.reshape(arm_count, slot_depth), "dp", split_axis=0, concat_axis=0, tiled=True
        ),
    )
    row_partial = returned.reshape(slot_total, full_width)[slot_index]
    grad_rep = lax.psum_scatter(
        row_partial.astype(jnp.float32).astype(jnp.bfloat16),
        "tower",
        scatter_dimension=1,
        tiled=True,
    )
    predicted = pred_back.reshape(slot_total)[slot_index]
    return (
        grad_matrix[None],
        grad_bias[None],
        grad_vector[None],
        grad_scalar.reshape(1),
        grad_rep,
        predicted,
    )


def solution(mesh):
    return jax.shard_map(
        body,
        mesh=mesh,
        in_specs=(
            P("dp", "tower"),
            P("dp"),
            P("dp"),
            P("dp"),
            P("dp", None, "tower"),
            P("dp", "tower"),
            P("dp", "tower"),
            P("dp"),
        ),
        out_specs=(
            P("dp", None, "tower"),
            P("dp", "tower"),
            P("dp", "tower"),
            P("dp"),
            P("dp", "tower"),
            P("dp"),
        ),
        check_vma=False,
    )
```

profile of v0, /device:TPU:8, one launch (start us, length us, event | category | flops | bytes accessed | tf_op | source)
XLA Modules:
  0.0 430.2 jit_solution(11687043676716487167)
XLA Ops:
  7.2 0.0 copy-start
  7.2 0.0 all-gather.2.cloned.1.call-start
  7.2 0.7 all-gather.2.cloned.1.call-update
  7.9 0.7 fusion.7
  8.6 0.6 reduce-window.6
  9.2 0.2 slice_reduce_fusion
  9.4 0.7 stack.10
  10.1 0.7 stack.9
  10.8 0.1 copy.25
  11.0 0.8 fusion.6
  11.7 0.7 compare_select_fusion.1
  12.4 1.4 scatter_custom_fusion
  13.9 2.4 gather_fusion.1
  16.3 0.1 copy.26
  16.4 0.2 reshape.61
  16.6 0.7 copy.27
  17.2 16.6 %all-to-all-start.1 = ((bf16[64,14,2]{1,2,0:T(2,128)(2,1)}), bf16[64,14,2]{1,2,0:T(2,128)(2,1)S(1)}, u32[]{:S(2)}, u32[]{:S(2)}) async-start(bf16[64,14,2]{1,2,0:T(2,128)(2,1)} %copy.27), calls=%async_computation.1 | async-start | bytes 65536 | tf_op jit(solution)/shard_map/all_to_all | solution.py:64
  33.8 9.6 %all-gather.2.cloned.1.call-done = bf16[256,2048]{1,0:T(8,128)(2,1)} async-done(((bf16[256,256]{1,0:T(8,128)(2,1)}), bf16[256,2048]{1,0:T(8,128)(2,1)}) %all-gather.2.cloned.1.call-update) | async-done | bytes 1048592 | tf_op jit(solution)/shard_map/all_gather | solution.py:58
  43.4 1.3 concatenate.6
  44.7 5.0 %gather_fusion = bf16[896,2048]{1,0:T(8,128)(2,1)} fusion(bf16[257,2048]{1,0:T(8,128)(2,1)S(1)} %concatenate.6, s32[1024]{0:T(1024)S(1)} %pad_clamp_fusion.1), kind=kCustom, calls=%fused_computation | custom fusion | bytes 7343616 | tf_op jit(solution)/shard_map/gather | solution.py:24
  49.8 6.0 %reshape.59 = bf16[64,14,2048]{2,1,0:T(8,128)(2,1)} reshape(bf16[896,2048]{1,0:T(8,128)(2,1)} %gather_fusion) | data formatting | bytes 7340032 | tf_op jit(solution)/shard_map/reshape | solution.py:59
  55.8 0.0 all-to-all-done.1
  55.8 13.6 %all-to-all-start = ((bf16[64,14,2048]{2,1,0:T(8,128)(2,1)}), bf16[64,14,2048]{2,1,0:T(8,128)(2,1)}, u32[]{:S(2)}, u32[]{:S(2)}) async-start(bf16[64,14,2048]{2,1,0:T(8,128)(2,1)} %reshape.59), calls=%async_computation | async-start | bytes 8388608 | tf_op jit(solution)/shard_map/all_to_all | solution.py:63
  70.0 0.1 copy.28
  70.1 0.1 copy.29
  70.2 0.1 reshape.66
  70.4 0.0 copy-start.1
  70.4 0.0 copy-start.2
  70.4 127.5 %all-to-all-done = bf16[64,14,2048]{2,1,0:T(8,128)(2,1)} async-done(((bf16[64,14,2048]{2,1,0:T(8,128)(2,1)}), bf16[64,14,2048]{2,1,0:T(8,128)(2,1)}, u32[]{:S(2)}, u32[]{:S(2)}) %all-to-all-start) | async-done | bytes 3670048 | tf_op jit(solution)/shard_map/all_to_all | solution.py:63
  197.9 5.8 %reshape.60 = bf16[896,2048]{1,0:T(8,128)(2,1)} reshape(bf16[64,14,2048]{2,1,0:T(8,128)(2,1)} %all-to-all-done) | data formatting | bytes 7340032 | tf_op jit(solution)/shard_map/reshape | solution.py:66
  203.8 0.0 copy-done
  203.8 0.0 copy-done.1
  203.8 0.0 copy-done.2
  203.8 3.3 multiply_reduce_fusion.1
  207.1 12.4 %psum.7 = f32[896]{0:T(1024)S(1)} all-reduce(f32[896]{0:T(1024)S(1)} %get-tuple-element.13), channel_id=1, replica_groups=mesh['dp'=64,'tower'=8] {'tower'}, use_global_device_ids=true, to_apply=%region_5.6 | all-reduce | flops 896 | bytes 7168 | tf_op jit(solution)/shard_map/psum | solution.py:32
  219.5 0.6 fusion.11
  220.1 3.1 convolution_convert_fusion
  223.2 6.0 %reshape.63 = bf16[64,14,2048]{2,1,0:T(8,128)(2,1)} reshape(bf16[896,2048]{1,0:T(8,128)(2,1)} %convolution_convert_fusion) | data formatting | bytes 7340032 | tf_op jit(solution)/shard_map/reshape | solution.py:80
  229.2 16.0 %all-to-all-start.2 = ((bf16[64,14,2048]{2,1,0:T(8,128)(2,1)}), bf16[64,14,2048]{2,1,0:T(8,128)(2,1)}, u32[]{:S(2)}, u32[]{:S(2)}) async-start(bf16[64,14,2048]{2,1,0:T(8,128)(2,1)} %reshape.63), calls=%async_computation.2 | async-start | bytes 8388608 | tf_op jit(solution)/shard_map/all_to_all | solution.py:79
  245.2 0.2 reduce-scatter.2.cloned.1.call-start
  245.4 123.7 %all-to-all-done.2 = bf16[64,14,2048]{2,1,0:T(8,128)(2,1)} async-done(((bf16[64,14,2048]{2,1,0:T(8,128)(2,1)}), bf16[64,14,2048]{2,1,0:T(8,128)(2,1)}, u32[]{:S(2)}, u32[]{:S(2)}) %all-to-all-start.2) | async-done | bytes 3670048 | tf_op jit(solution)/shard_map/all_to_all | solution.py:79
  369.1 6.0 %reshape.64 = bf16[896,2048]{1,0:T(8,128)(2,1)} reshape(bf16[64,14,2048]{2,1,0:T(8,128)(2,1)} %all-to-all-done.2) | data formatting | bytes 7340032 | tf_op jit(solution)/shard_map/reshape | solution.py:90
  375.1 5.9 %gather_fusion.2 = bf16[256,2048]{1,0:T(8,128)(2,1)} fusion(bf16[896,2048]{1,0:T(8,128)(2,1)} %reshape.64, s32[1024]{0:T(1024)S(1)} %pad_clamp_fusion), kind=kCustom, calls=%fused_computation.2 | custom fusion | bytes 2098176 | tf_op jit(solution)/shard_map/gather | solution.py:90
  380.9 0.0 reduce-scatter.2.cloned.1.call-update
  380.9 0.8 all_to_all.20
  381.7 13.4 %all-to-all-start.3 = ((bf16[64,1,14]{2,1,0:T(2,128)(2,1)}), bf16[64,1,14]{2,1,0:T(2,128)(2,1)S(1)}, u32[]{:S(2)}, u32[]{:S(2)}) async-start(bf16[64,1,14]{2,1,0:T(2,128)(2,1)} %all_to_all.20), calls=%async_computation.4 | async-start | bytes 65536 | tf_op jit(solution)/shard_map/all_to_all | solution.py:86
  395.1 4.9 %convolution_bitcast_fusion = f32[1,2048,256]{2,1,0:T(8,128)} fusion(bf16[896,2048]{1,0:T(8,128)(2,1)} %reshape.60, f32[896,256]{1,0:T(8,128)S(1)} %get-tuple-element.14, f32[896]{0:T(1024)S(1)} %get-tuple-element.11, f32[256]{0:T(256)S(1)} %bitcast.41), kind=kOutput, calls=%fused_computation.6 | convolution fusion | flops 941817856 | bytes 6689280 | tf_op jit(solution)/shard_map/dot_general | solution.py:36
  400.0 1.1 multiply_reduce_fusion
  401.1 5.0 %all-to-all-done.3 = bf16[64,1,14]{2,1,0:T(2,128)(2,1)S(1)} async-done(((bf16[64,1,14]{2,1,0:T(2,128)(2,1)}), bf16[64,1,14]{2,1,0:T(2,128)(2,1)S(1)}, u32[]{:S(2)}, u32[]{:S(2)}) %all-to-all-start.3) | async-done | bytes 1824 | tf_op jit(solution)/shard_map/all_to_all | solution.py:86
  406.1 0.1 reduce.3
  406.2 0.1 reshape.65
  406.3 2.4 gather_fusion.3
  408.8 14.5 %reduce-scatter.2.cloned.1.call-done = bf16[256,256]{1,0:T(8,128)(2,1)} async-done(((bf16[256,2048]{1,0:T(8,128)(2,1)}), bf16[256,256]{1,0:T(8,128)(2,1)}) %reduce-scatter.2.cloned.1.call-update) | async-done | bytes 131088 | tf_op jit(solution)/shard_map/reduce_scatter | solution.py:91
  (9 shorter events, 0.1 us)
Async XLA Ops:
  7.2 196.6 %copy-start = (bf16[1,2048,256]{2,1,0:T(8,128)(2,1)S(1)}, bf16[1,2048,256]{2,1,0:T(8,128)(2,1)}, u32[]{:S(2)}) copy-start(bf16[1,2048,256]{2,1,0:T(8,128)(2,1)} %param.12) | copy-start | bytes 3145732
  7.2 36.3 %all-gather.2.cloned.1.call-start = ((), (), s32[]{:S(2)}) async-start(), calls=%async_computation.5 | async-start | bytes 1179648 | tf_op jit(solution)/shard_map/all_gather | solution.py:58
  17.2 38.5 %all-to-all-start.1 = ((bf16[64,14,2]{1,2,0:T(2,128)(2,1)}), bf16[64,14,2]{1,2,0:T(2,128)(2,1)S(1)}, u32[]{:S(2)}, u32[]{:S(2)}) async-start(bf16[64,14,2]{1,2,0:T(2,128)(2,1)} %copy.27), calls=%async_computation.1 | async-start | bytes 65536 | tf_op jit(solution)/shard_map/all_to_all | solution.py:64
  55.8 142.2 %all-to-all-start = ((bf16[64,14,2048]{2,1,0:T(8,128)(2,1)}), bf16[64,14,2048]{2,1,0:T(8,128)(2,1)}, u32[]{:S(2)}, u32[]{:S(2)}) async-start(bf16[64,14,2048]{2,1,0:T(8,128)(2,1)} %reshape.59), calls=%async_computation | async-start | bytes 8388608 | tf_op jit(solution)/shard_map/all_to_all | solution.py:63
  70.4 133.4 %copy-start.1 = (f32[1,256]{1,0:T(1,128)S(1)}, f32[1,256]{1,0:T(1,128)}, u32[]{:S(2)}) copy-start(f32[1,256]{1,0:T(1,128)} %param.14) | copy-start | bytes 3076
  70.4 133.4 %copy-start.2 = (f32[1,256]{1,0:T(1,128)S(1)}, f32[1,256]{1,0:T(1,128)}, u32[]{:S(2)}) copy-start(f32[1,256]{1,0:T(1,128)} %param.13) | copy-start | bytes 3076
  229.2 139.9 %all-to-all-start.2 = ((bf16[64,14,2048]{2,1,0:T(8,128)(2,1)}), bf16[64,14,2048]{2,1,0:T(8,128)(2,1)}, u32[]{:S(2)}, u32[]{:S(2)}) async-start(bf16[64,14,2048]{2,1,0:T(8,128)(2,1)} %reshape.63), calls=%async_computation.2 | async-start | bytes 8388608 | tf_op jit(solution)/shard_map/all_to_all | solution.py:79
  245.2 178.2 %reduce-scatter.2.cloned.1.call-start = ((), (), s32[]{:S(2)}) async-start(), calls=%async_computation.6 | async-start | bytes 1179648 | tf_op jit(solution)/shard_map/reduce_scatter | solution.py:91
  381.7 24.4 %all-to-all-start.3 = ((bf16[64,1,14]{2,1,0:T(2,128)(2,1)}), bf16[64,1,14]{2,1,0:T(2,128)(2,1)S(1)}, u32[]{:S(2)}, u32[]{:S(2)}) async-start(bf16[64,1,14]{2,1,0:T(2,128)(2,1)} %all_to_all.20), calls=%async_computation.4 | async-start | bytes 65536 | tf_op jit(solution)/shard_map/all_to_all | solution.py:86
Sparse Core Ops, SparseCore 0:
  10.1 33.2 all-gather.1
  381.1 42.2 reduce-scatter.1
where the time goes:
time: 431 us; the launch traced here: 430 us
  waiting for transfers between devices  281 us (65%)
  starting transfers between devices  59.7 us (14%)
  local copies, waits for them, and re-layouts  46.2 us (11%)
  between operations  14.8 us (3%)
  blocking collectives  12.4 us (3%)
  matrix products  11.3 us (3%)
  other arithmetic  4.59 us (1%)
    all_to_all x1, waiting for transfers between devices, body(): lax.all_to_all(wide_slots, 'dp', split_axis=0, concat_axis=0, tiled=True)  128 us
    all_to_all x1, waiting for transfers between devices, body(): lax.all_to_all(partial_full.reshape(arm_count, slot_depth, full_width), '...  124 us
    all_to_all x1, starting transfers between devices, body(): lax.all_to_all(side_data, 'dp', split_axis=0, concat_axis=0, tiled=True)  16.6 us
    all_to_all x1, starting transfers between devices, body(): lax.all_to_all(partial_full.reshape(arm_count, slot_depth, full_width), '...  16 us
    reduce_scatter x1, waiting for transfers between devices, body(): lax.psum_scatter(row_partial.astype(jnp.float32).astype(jnp.bfloat16), 't...  14.5 us
    all_to_all x1, starting transfers between devices, body(): lax.all_to_all(wide_slots, 'dp', split_axis=0, concat_axis=0, tiled=True)  13.6 us
    all_to_all x1, starting transfers between devices, body(): lax.all_to_all(pred_half.reshape(arm_count, slot_depth), 'dp', split_axis...  13.4 us
    psum x1, blocking collectives, tower_step(): full_pred = lax.psum(pred_share, 'tower') + head_bias  12.4 us
  transfers between devices with their start and end apart: 6, of which 5 were waited for; matrix products, arithmetic and copies ran while one was open for 7% of the time, Pallas kernels for 0%

commit v1 on v0

--- a/solution.py
+++ b/solution.py
@@ -55,7 +55,8 @@
     bias_cols = b_hidden[0]
     head_cols = w_head[0]
     head_bias = b_head[0]
-    wide_rep = lax.all_gather(rep, "tower", axis=1, tiled=True)
+    repeated = jnp.stack([rep] * lax.axis_size("tower"))
+    wide_rep = jnp.concatenate(lax.all_to_all(repeated, "tower", 0, 0), axis=1)
     wide_slots = fill_slots(wide_rep, slot_index, slot_total).reshape(
         arm_count, slot_depth, wide_rep.shape[1]
     )

time: 431 us -> 435 us (level)
  starting transfers between devices: 59.7 us -> 64.8 us
    all_gather x1 -> x0, waiting for transfers between devices: 9.63 us -> none  [body(): wide_rep = lax.all_gather(rep, 'tower', axis=1, tiled=True)]
    all_to_all x0 -> x1, waiting for transfers between devices: none -> 8 us  [body(): wide_rep = jnp.concatenate(lax.all_to_all(repeated, 'tower', 0, 0), axis=1)]
where the time goes in v1:
time: 435 us; the launch traced here: 434 us
  waiting for transfers between devices  280 us (64%)
  starting transfers between devices  64.8 us (15%)
  local copies, waits for them, and re-layouts  47.1 us (11%)
  between operations  14.9 us (3%)
  blocking collectives  12.4 us (3%)
  matrix products  11.4 us (3%)
    all_to_all x1, waiting for transfers between devices, body(): lax.all_to_all(wide_slots, 'dp', split_axis=0, concat_axis=0, tiled=True)  130 us
    all_to_all x1, waiting for transfers between devices, body(): lax.all_to_all(partial_full.reshape(arm_count, slot_depth, full_width), '...  120 us
    all_to_all x1, starting transfers between devices, body(): lax.all_to_all(pred_half.reshape(arm_count, slot_depth), 'dp', split_axis...  17.6 us
    reduce_scatter x1, waiting for transfers between devices, body(): lax.psum_scatter(row_partial.astype(jnp.float32).astype(jnp.bfloat16), 't...  16.7 us
    all_to_all x1, starting transfers between devices, body(): lax.all_to_all(side_data, 'dp', split_axis=0, concat_axis=0, tiled=True)  16.6 us
    all_to_all x1, starting transfers between devices, body(): lax.all_to_all(partial_full.reshape(arm_count, slot_depth, full_width), '...  13.2 us
    all_to_all x1, starting transfers between devices, body(): lax.all_to_all(wide_slots, 'dp', split_axis=0, concat_axis=0, tiled=True)  12.9 us
    psum x1, blocking collectives, tower_step(): full_pred = lax.psum(pred_share, 'tower') + head_bias  12.4 us
  transfers between devices with their start and end apart: 6, of which 5 were waited for; matrix products, arithmetic and copies ran while one was open for 7% of the time, Pallas kernels for 0%

profile of v1, /device:TPU:8, one launch (start us, length us, event | category | flops | bytes accessed | tf_op | source)
XLA Modules:
  0.0 433.6 jit_solution(12433955735760482851)
XLA Ops:
  7.2 0.0 copy-start
  7.2 0.0 copy-start.1
  7.2 2.0 stack.8
  9.2 4.3 all-to-all-start
  13.5 0.7 fusion.7
  14.2 0.6 reduce-window.6
  14.8 0.2 slice_reduce_fusion
  15.0 0.7 stack.10
  15.7 0.7 stack.9
  16.4 0.1 copy.27
  16.6 0.0 copy-done.1
  16.6 0.1 fusion.6
  16.7 1.4 scatter_custom_fusion
  18.1 2.4 gather_fusion.1
  20.5 0.1 copy.28
  20.7 0.2 reshape.71
  20.8 0.7 copy.29
  21.5 8.0 %all-to-all-done = bf16[8,256,256]{2,1,0:T(8,128)(2,1)S(1)} async-done(((bf16[8,256,256]{2,1,0:T(8,128)(2,1)}), bf16[8,256,256]{2,1,0:T(8,128)(2,1)S(1)}, u32[]{:S(2)}, u32[]{:S(2)}) %all-to-all-start) | async-done | bytes 1048608 | tf_op jit(solution)/shard_map/all_to_all | solution.py:59
  29.5 16.6 %all-to-all-start.2 = ((bf16[64,14,2]{1,2,0:T(2,128)(2,1)}), bf16[64,14,2]{1,2,0:T(2,128)(2,1)S(1)}, u32[]{:S(2)}, u32[]{:S(2)}) async-start(bf16[64,14,2]{1,2,0:T(2,128)(2,1)} %copy.29), calls=%async_computation.2 | async-start | bytes 65536 | tf_op jit(solution)/shard_map/all_to_all | solution.py:65
  46.1 0.1 copy.33
  46.2 0.1 concatenate.6
  46.3 5.0 %gather_fusion = bf16[896,2048]{1,0:T(8,128)(2,1)} fusion(bf16[257,2048]{1,0:T(8,128)(2,1)S(1)} %concatenate.6, s32[1024]{0:T(1024)S(1)} %pad_clamp_fusion.1), kind=kCustom, calls=%fused_computation | custom fusion | bytes 7343616 | tf_op jit(solution)/shard_map/gather | solution.py:24
  51.3 6.0 %reshape.69 = bf16[64,14,2048]{2,1,0:T(8,128)(2,1)} reshape(bf16[896,2048]{1,0:T(8,128)(2,1)} %gather_fusion) | data formatting | bytes 7340032 | tf_op jit(solution)/shard_map/reshape | solution.py:60
  57.3 0.0 all-to-all-done.2
  57.3 12.9 %all-to-all-start.1 = ((bf16[64,14,2048]{2,1,0:T(8,128)(2,1)}), bf16[64,14,2048]{2,1,0:T(8,128)(2,1)}, u32[]{:S(2)}, u32[]{:S(2)}) async-start(bf16[64,14,2048]{2,1,0:T(8,128)(2,1)} %reshape.69), calls=%async_computation.1 | async-start | bytes 8388608 | tf_op jit(solution)/shard_map/all_to_all | solution.py:64
  70.9 0.1 copy.30
  71.0 0.1 copy.31
  71.1 0.1 reshape.76
  71.3 0.0 copy-start.2
  71.3 0.0 copy-start.3
  71.3 130.3 %all-to-all-done.1 = bf16[64,14,2048]{2,1,0:T(8,128)(2,1)} async-done(((bf16[64,14,2048]{2,1,0:T(8,128)(2,1)}), bf16[64,14,2048]{2,1,0:T(8,128)(2,1)}, u32[]{:S(2)}, u32[]{:S(2)}) %all-to-all-start.1) | async-done | bytes 3670048 | tf_op jit(solution)/shard_map/all_to_all | solution.py:64
  201.6 5.8 %reshape.70 = bf16[896,2048]{1,0:T(8,128)(2,1)} reshape(bf16[64,14,2048]{2,1,0:T(8,128)(2,1)} %all-to-all-done.1) | data formatting | bytes 7340032 | tf_op jit(solution)/shard_map/reshape | solution.py:67
  207.5 0.0 copy-done
  207.5 0.0 copy-done.2
  207.5 0.0 copy-done.3
  207.5 3.3 multiply_reduce_fusion.1
  210.8 12.4 %psum.7 = f32[896]{0:T(1024)S(1)} all-reduce(f32[896]{0:T(1024)S(1)} %get-tuple-element.13), channel_id=1, replica_groups=mesh['dp'=64,'tower'=8] {'tower'}, use_global_device_ids=true, to_apply=%region_5.6 | all-reduce | flops 896 | bytes 7168 | tf_op jit(solution)/shard_map/psum | solution.py:32
  223.2 0.6 fusion.11
  223.8 3.1 convolution_convert_fusion
  226.9 6.0 %reshape.73 = bf16[64,14,2048]{2,1,0:T(8,128)(2,1)} reshape(bf16[896,2048]{1,0:T(8,128)(2,1)} %convolution_convert_fusion) | data formatting | bytes 7340032 | tf_op jit(solution)/shard_map/reshape | solution.py:81
  232.9 13.2 %all-to-all-start.3 = ((bf16[64,14,2048]{2,1,0:T(8,128)(2,1)}), bf16[64,14,2048]{2,1,0:T(8,128)(2,1)}, u32[]{:S(2)}, u32[]{:S(2)}) async-start(bf16[64,14,2048]{2,1,0:T(8,128)(2,1)} %reshape.73), calls=%async_computation.3 | async-start | bytes 8388608 | tf_op jit(solution)/shard_map/all_to_all | solution.py:80
  246.1 0.2 reduce-scatter.2.cloned.1.call-start
  246.4 119.7 %all-to-all-done.3 = bf16[64,14,2048]{2,1,0:T(8,128)(2,1)} async-done(((bf16[64,14,2048]{2,1,0:T(8,128)(2,1)}), bf16[64,14,2048]{2,1,0:T(8,128)(2,1)}, u32[]{:S(2)}, u32[]{:S(2)}) %all-to-all-start.3) | async-done | bytes 3670048 | tf_op jit(solution)/shard_map/all_to_all | solution.py:80
  366.1 6.0 %reshape.74 = bf16[896,2048]{1,0:T(8,128)(2,1)} reshape(bf16[64,14,2048]{2,1,0:T(8,128)(2,1)} %all-to-all-done.3) | data formatting | bytes 7340032 | tf_op jit(solution)/shard_map/reshape | solution.py:91
  372.1 5.9 %gather_fusion.2 = bf16[256,2048]{1,0:T(8,128)(2,1)} fusion(bf16[896,2048]{1,0:T(8,128)(2,1)} %reshape.74, s32[1024]{0:T(1024)S(1)} %pad_clamp_fusion), kind=kCustom, calls=%fused_computation.2 | custom fusion | bytes 2098176 | tf_op jit(solution)/shard_map/gather | solution.py:91
  377.9 0.0 reduce-scatter.2.cloned.1.call-update
  377.9 0.8 all_to_all.24
  378.7 17.6 %all-to-all-start.4 = ((bf16[64,1,14]{2,1,0:T(2,128)(2,1)}), bf16[64,1,14]{2,1,0:T(2,128)(2,1)S(1)}, u32[]{:S(2)}, u32[]{:S(2)}) async-start(bf16[64,1,14]{2,1,0:T(2,128)(2,1)} %all_to_all.24), calls=%async_computation.5 | async-start | bytes 65536 | tf_op jit(solution)/shard_map/all_to_all | solution.py:87
  396.3 4.9 %convolution_bitcast_fusion = f32[1,2048,256]{2,1,0:T(8,128)} fusion(bf16[896,2048]{1,0:T(8,128)(2,1)} %reshape.70, f32[896,256]{1,0:T(8,128)S(1)} %get-tuple-element.14, f32[896]{0:T(1024)S(1)} %get-tuple-element.11, f32[256]{0:T(256)S(1)} %bitcast.46), kind=kOutput, calls=%fused_computation.6 | convolution fusion | flops 941817856 | bytes 6689280 | tf_op jit(solution)/shard_map/dot_general | solution.py:36
  401.2 1.1 multiply_reduce_fusion
  402.3 5.0 %all-to-all-done.4 = bf16[64,1,14]{2,1,0:T(2,128)(2,1)S(1)} async-done(((bf16[64,1,14]{2,1,0:T(2,128)(2,1)}), bf16[64,1,14]{2,1,0:T(2,128)(2,1)S(1)}, u32[]{:S(2)}, u32[]{:S(2)}) %all-to-all-start.4) | async-done | bytes 1824 | tf_op jit(solution)/shard_map/all_to_all | solution.py:87
  407.3 0.1 reduce.3
  407.4 0.1 reshape.75
  407.6 2.4 gather_fusion.3
  410.0 16.7 %reduce-scatter.2.cloned.1.call-done = bf16[256,256]{1,0:T(8,128)(2,1)} async-done(((bf16[256,2048]{1,0:T(8,128)(2,1)}), bf16[256,256]{1,0:T(8,128)(2,1)}) %reduce-scatter.2.cloned.1.call-update) | async-done | bytes 131088 | tf_op jit(solution)/shard_map/reduce_scatter | solution.py:92
  (10 shorter events, 0.1 us)
Async XLA Ops:
  7.2 200.3 %copy-start = (bf16[1,2048,256]{2,1,0:T(8,128)(2,1)S(1)}, bf16[1,2048,256]{2,1,0:T(8,128)(2,1)}, u32[]{:S(2)}) copy-start(bf16[1,2048,256]{2,1,0:T(8,128)(2,1)} %param.12) | copy-start | bytes 3145732
  7.2 9.4 %copy-start.1 = (s32[256]{0:T(256)S(1)}, s32[256]{0:T(256)}, u32[]{:S(2)}) copy-start(s32[256]{0:T(256)} %param.9) | copy-start | bytes 3076
  9.2 20.3 %all-to-all-start = ((bf16[8,256,256]{2,1,0:T(8,128)(2,1)}), bf16[8,256,256]{2,1,0:T(8,128)(2,1)S(1)}, u32[]{:S(2)}, u32[]{:S(2)}) async-start(bf16[8,256,256]{2,1,0:T(8,128)(2,1)} %stack.8), calls=%async_computation | async-start | bytes 2097152 | tf_op jit(solution)/shard_map/all_to_all | solution.py:59
  29.5 27.8 %all-to-all-start.2 = ((bf16[64,14,2]{1,2,0:T(2,128)(2,1)}), bf16[64,14,2]{1,2,0:T(2,128)(2,1)S(1)}, u32[]{:S(2)}, u32[]{:S(2)}) async-start(bf16[64,14,2]{1,2,0:T(2,128)(2,1)} %copy.29), calls=%async_computation.2 | async-start | bytes 65536 | tf_op jit(solution)/shard_map/all_to_all | solution.py:65
  57.3 144.3 %all-to-all-start.1 = ((bf16[64,14,2048]{2,1,0:T(8,128)(2,1)}), bf16[64,14,2048]{2,1,0:T(8,128)(2,1)}, u32[]{:S(2)}, u32[]{:S(2)}) async-start(bf16[64,14,2048]{2,1,0:T(8,128)(2,1)} %reshape.69), calls=%async_computation.1 | async-start | bytes 8388608 | tf_op jit(solution)/shard_map/all_to_all | solution.py:64
  71.3 136.2 %copy-start.2 = (f32[1,256]{1,0:T(1,128)S(1)}, f32[1,256]{1,0:T(1,128)}, u32[]{:S(2)}) copy-start(f32[1,256]{1,0:T(1,128)} %param.14) | copy-start | bytes 3076
  71.3 136.2 %copy-start.3 = (f32[1,256]{1,0:T(1,128)S(1)}, f32[1,256]{1,0:T(1,128)}, u32[]{:S(2)}) copy-start(f32[1,256]{1,0:T(1,128)} %param.13) | copy-start | bytes 3076
  232.9 133.2 %all-to-all-start.3 = ((bf16[64,14,2048]{2,1,0:T(8,128)(2,1)}), bf16[64,14,2048]{2,1,0:T(8,128)(2,1)}, u32[]{:S(2)}, u32[]{:S(2)}) async-start(bf16[64,14,2048]{2,1,0:T(8,128)(2,1)} %reshape.73), calls=%async_computation.3 | async-start | bytes 8388608 | tf_op jit(solution)/shard_map/all_to_all | solution.py:80
  246.1 180.6 %reduce-scatter.2.cloned.1.call-start = ((), (), s32[]{:S(2)}) async-start(), calls=%async_computation.6 | async-start | bytes 1179648 | tf_op jit(solution)/shard_map/reduce_scatter | solution.py:92
  378.7 28.6 %all-to-all-start.4 = ((bf16[64,1,14]{2,1,0:T(2,128)(2,1)}), bf16[64,1,14]{2,1,0:T(2,128)(2,1)S(1)}, u32[]{:S(2)}, u32[]{:S(2)}) async-start(bf16[64,1,14]{2,1,0:T(2,128)(2,1)} %all_to_all.24), calls=%async_computation.5 | async-start | bytes 65536 | tf_op jit(solution)/shard_map/all_to_all | solution.py:87
Sparse Core Ops, SparseCore 0:
  378.1 48.6 reduce-scatter.1
